TPU v7x, 32 devices: a whole 2x2x4 slice. The times are simulated.
32 devices in a mesh: groups: 2 (over x), query: 16 (over z, y, core).
Axes of the slice: x: 2, y: 2, z: 4, core: 2. Of those that a mesh axis runs over, the one named last changes fastest.
Arguments:
- tokens: bfloat16 [384, 4096], P(('groups', 'query')), parts along dimension 0, may hold values from -6 to 6
- grad_out: bfloat16 [384, 4096], P(('groups', 'query')), parts along dimension 0, may hold values from -6 to 6
- gate_weight: bfloat16 [4096, 14336], P(None, 'query'), may hold values from -0.09375 to 0.09375
- up_weight: bfloat16 [4096, 14336], P(None, 'query'), may hold values from -0.09375 to 0.09375
- query_left: bfloat16 [16, 4096, 32], P('query'), may hold values from -0.09375 to 0.09375
- query_right: bfloat16 [16, 14336, 32], P('query'), may hold values from -0.09375 to 0.09375
Outputs:
- scores: float32 [384, 16], P(('groups', 'query')), parts along dimension 0
There are 2 independent parts, one for each index of `groups`. A program takes and returns all parts, laid end to end along the dimension named above; an argument that names none is the same for every part. Nothing has to cross between parts.
All inputs are finite; a program needn't handle non-finite values.
Results may differ from a plain program's by a relative error of at most 0.0003.
Values may be sent and summed in bfloat16 or wider, within the bound.
No kernel may reach another device: no remote copies, remote signals or barrier semaphores. Data moves between devices by JAX's collectives and lax.ppermute only.
A program may use at most 128 MiB of HBM per device.

v0:
```python
import jax
import jax.numpy as jnp
from jax import lax
from jax.sharding import PartitionSpec as P


def body(tokens, grad_out, gate_weight, up_weight, query_left, query_right):
    whole = lax.all_gather(tokens, "query", axis=0, tiled=True)
    right_cols = lax.all_to_all(query_right, "query", split_axis=1, concat_axis=0, tiled=True)
    right_wide = right_cols.astype(jnp.float32)
    num_queries = right_cols.shape[0]
    rank_size = right_cols.shape[2]
    tok_rows = tokens.shape[0]
    gate = jnp.dot(whole, gate_weight, preferred_element_type=jnp.float32)
    up = jnp.dot(whole, up_weight, preferred_element_type=jnp.float32)
    hidden = jax.nn.silu(gate) * up
    term = jnp.einsum("tf,qfr->tqr", hidden, right_wide, precision=lax.Precision.HIGHEST)
    proj_right = lax.psum_scatter(
        term.reshape(tok_rows * lax.axis_size("query"), num_queries * rank_size),
        "query",
        scatter_dimension=0,
        tiled=True,
    )
    proj_right = proj_right.reshape(tok_rows, num_queries, rank_size)
    left = jnp.einsum(
        "td,kdr->tkr",
        grad_out,
        lax.all_gather(query_left, "query", axis=0, tiled=True),
        preferred_element_type=jnp.float32,
    )
    return jnp.sum(left * proj_right, axis=2)


def solution(mesh):
    return jax.shard_map(
        body,
        mesh=mesh,
        in_specs=(
            P(("groups", "query"), None),
            P(("groups", "query"), None),
            P(None, "query"),
            P(None, "query"),
            P("query", None, None),
            P("query", None, None),
        ),
        out_specs=P(("groups", "query"), None),
        check_vma=False,
    )
```

profile of v0, /device:TPU:17, one launch (start us, length us, event | category | flops | bytes accessed | tf_op | source)
XLA Modules:
  0.0 230.3 jit_solution(11249629762622206637)
XLA Ops:
  6.5 0.0 copy-start
  6.5 0.0 all-gather.6.cloned.1.call-start
  6.5 0.7 all-gather.6.cloned.1.call-update
  7.3 0.0 all-gather.4.cloned.1.call-start
  7.3 0.7 all-gather.4.cloned.1.call-update
  8.0 14.3 %copy.10 = bf16[1,14336,32]{2,0,1:T(2,128)(2,1)} copy(bf16[1,14336,32]{1,2,0:T(8,128)(2,1)} %param.11) | data formatting | bytes 1835008 | tf_op args[5]
  22.3 0.5 broadcast.2
  22.8 79.8 %reduce = bf16[14336,32]{1,0:T(8,128)(2,1)} reduce(bf16[14336,1,32]{2,1,0:T(2,128)(2,1)} %bitcast.26, bf16[]{:T(256)} %broadcast.2), dimensions={1}, to_apply=%bitcast.15.reduce_sub_computation | reduce | bytes 1835010
  102.6 5.0 %reshape.13 = bf16[16,2,14336]{2,1,0:T(2,128)(2,1)S(1)} reshape(bf16[14336,32]{1,0:T(8,128)(2,1)} %reduce) | data formatting | bytes 1835008
  107.5 27.9 %all_to_all.12 = bf16[16,2,14336]{2,1,0:T(2,128)(2,1)S(1)} all-to-all(bf16[16,2,14336]{2,1,0:T(2,128)(2,1)S(1)} %reshape.13), channel_id=1, replica_groups=mesh['groups'=2,'query'=16] {'query'}, dimensions={0} | all-to-all | bytes 1835008 | tf_op jit(solution)/shard_map/all_to_all | solution.py:9
  135.4 8.4 %reshape.14 = bf16[14336,1,32]{2,1,0:T(2,128)(2,1)} reshape(bf16[16,2,14336]{2,1,0:T(2,128)(2,1)S(1)} %all_to_all.12) | data formatting | bytes 1835008
  143.8 13.7 %copy.11 = bf16[1,14336,32]{1,2,0:T(8,128)(2,1)S(1)} copy(bf16[1,14336,32]{2,0,1:T(2,128)(2,1)} %bitcast.27) | data formatting | bytes 1835008 | tf_op jit(solution)/shard_map/all_to_all | solution.py:9
  157.5 0.1 copy.15
  157.6 0.2 copy.12
  157.8 0.0 all-gather.6.cloned.1.call-done
  157.8 2.5 %reshape.10 = bf16[192,4096]{1,0:T(8,128)(2,1)S(1)} reshape(bf16[16,12,4096]{2,1,0:T(8,128)(2,1)} %all-gather.6.cloned.1.call-done) | data formatting | bytes 3145728
  160.3 4.9 %fusion.4 = f32[192,896]{1,0:T(8,128)S(1)} fusion(bf16[192,4096]{1,0:T(8,128)(2,1)S(1)} %reshape.10, bf16[4096,896]{1,0:T(8,128)(2,1)} %param.8), kind=kOutput, calls=%fused_computation.6 | convolution fusion | flops 1409286144 | bytes 9601024 | tf_op jit(solution)/shard_map/dot_general | solution.py:14
  165.2 0.0 copy-start.1
  165.2 4.9 %convolution_multiply_fusion = f32[192,896]{1,0:T(8,128)S(1)} fusion(bf16[192,4096]{1,0:T(8,128)(2,1)S(1)} %reshape.10, bf16[4096,896]{1,0:T(8,128)(2,1)} %param.9, f32[192,896]{1,0:T(8,128)S(1)} %fusion.4), kind=kOutput, calls=%fused_computation | convolution fusion | flops 1410146304 | bytes 10289152 | tf_op jit(solution)/shard_map/dot_general | solution.py:15
  170.1 1.1 fusion.5
  171.2 25.9 %fusion = f32[16,512]{1,0:T(8,128)S(1)} fusion(f32[192,512]{1,0:T(8,128)S(1)} %fusion.5), kind=kCustom, calls=%all-reduce-scatter | all-reduce-scatter fusion | flops 131073 | bytes 426496
  197.1 2.8 %collective-permute-start = (f32[16,512]{1,0:T(8,128)S(1)}, f32[16,512]{1,0:T(8,128)S(1)}, u32[]{:S(2)}, u32[]{:S(2)}) collective-permute-start(f32[16,512]{1,0:T(8,128)S(1)} %fusion), channel_id=1, source_target_pairs={{0,1},{1,2},{2,3},{3,4},{4,5},{5,6},{6,7},{7,8},{8,9},{9,10},{10,1... | collective-permute-start | bytes 98312
  199.9 5.0 %collective-permute-start.1 = (f32[16,512]{1,0:T(8,128)S(1)}, f32[16,512]{1,0:T(8,128)S(1)}, u32[]{:S(2)}, u32[]{:S(2)}) collective-permute-start(f32[16,512]{1,0:T(8,128)S(1)} %fusion), channel_id=1, source_target_pairs={{0,2},{1,3},{2,4},{3,5},{4,6},{5,7},{6,8},{7,9},{8,10},{9,11},{10,... | collective-permute-start | bytes 98312
  204.8 7.5 %collective-permute-start.2 = (f32[16,512]{1,0:T(8,128)S(1)}, f32[16,512]{1,0:T(8,128)S(1)}, u32[]{:S(2)}, u32[]{:S(2)}) collective-permute-start(f32[16,512]{1,0:T(8,128)S(1)} %fusion), channel_id=1, source_target_pairs={{0,3},{1,4},{2,5},{3,6},{4,7},{5,8},{6,9},{7,10},{8,11},{9,12},{10... | collective-permute-start | bytes 98312
  212.3 1.9 collective-permute-start.3
  214.2 0.0 copy-done.1
  214.3 0.6 dynamic-slice.4
  215.5 1.5 collective-permute-done.3
  217.0 0.0 collective-permute-done
  217.0 0.0 collective-permute-done.1
  217.0 0.0 collective-permute-done.2
  217.0 0.5 concatenate
  217.5 0.1 reshape.8
  217.6 0.0 all-gather.4.cloned.1.call-done
  217.6 0.0 copy-done
  217.6 5.1 %fusion.3 = f32[12,16]{0,1:T(8,128)S(1)} fusion(f32[12,16,32]{2,1,0:T(8,128)S(1)} %reshape.8, bf16[16,4096,32]{1,2,0:T(8,128)(2,1)} %all-gather.4.cloned.1.call-done, bf16[12,4096]{1,0:T(8,128)(2,1)S(1)} %copy-done), kind=kOutput, calls=%fused_computation.4 | convolution fusion | flops 50343744 | bytes 4317952 | tf_op jit(solution)/shard_map/td,kdr->tkr/dot_general | solution.py:25
  222.7 0.7 copy.14
  (2 shorter events, 0.0 us)
Async XLA Ops:
  6.5 211.1 %copy-start = (bf16[12,4096]{1,0:T(8,128)(2,1)S(1)}, bf16[12,4096]{1,0:T(8,128)(2,1)}, u32[]{:S(2)}) copy-start(bf16[12,4096]{1,0:T(8,128)(2,1)} %param.7) | copy-start | bytes 294916
  6.5 151.2 %all-gather.6.cloned.1.call-start = ((), (), s32[]{:S(2)}) async-start(), calls=%async_computation.2 | async-start | bytes 2228224 | tf_op jit(solution)/shard_map/all_gather | solution.py:8
  7.3 210.4 %all-gather.4.cloned.1.call-start = ((), (), s32[]{:S(2)}) async-start(), calls=%async_computation.1 | async-start | bytes 4456448 | tf_op jit(solution)/shard_map/all_gather | solution.py:28
  165.2 49.1 %copy-start.1 = (u32[32]{0:T(128)S(1)}, u32[32]{0:T(128)}, u32[]{:S(2)}) copy-start(u32[32]{0:T(128)} %constant.11) | copy-start | bytes 388
  197.1 19.9 %collective-permute-start = (f32[16,512]{1,0:T(8,128)S(1)}, f32[16,512]{1,0:T(8,128)S(1)}, u32[]{:S(2)}, u32[]{:S(2)}) collective-permute-start(f32[16,512]{1,0:T(8,128)S(1)} %fusion), channel_id=1, source_target_pairs={{0,1},{1,2},{2,3},{3,4},{4,5},{5,6},{6,7},{7,8},{8,9},{9,10},{10,1... | collective-permute-start | bytes 98312
  199.9 17.1 %collective-permute-start.1 = (f32[16,512]{1,0:T(8,128)S(1)}, f32[16,512]{1,0:T(8,128)S(1)}, u32[]{:S(2)}, u32[]{:S(2)}) collective-permute-start(f32[16,512]{1,0:T(8,128)S(1)} %fusion), channel_id=1, source_target_pairs={{0,2},{1,3},{2,4},{3,5},{4,6},{5,7},{6,8},{7,9},{8,10},{9,11},{10,... | collective-permute-start | bytes 98312
  204.8 12.1 %collective-permute-start.2 = (f32[16,512]{1,0:T(8,128)S(1)}, f32[16,512]{1,0:T(8,128)S(1)}, u32[]{:S(2)}, u32[]{:S(2)}) collective-permute-start(f32[16,512]{1,0:T(8,128)S(1)} %fusion), channel_id=1, source_target_pairs={{0,3},{1,4},{2,5},{3,6},{4,7},{5,8},{6,9},{7,10},{8,11},{9,12},{10... | collective-permute-start | bytes 98312
  212.3 4.7 %collective-permute-start.3 = (f32[12,512]{1,0:T(8,128)S(1)}, f32[12,512]{1,0:T(8,128)S(1)}, u32[]{:S(2)}, u32[]{:S(2)}) collective-permute-start(f32[12,512]{1,0:T(8,128)S(1)} %slice), channel_id=1, source_target_pairs={{0,4},{1,5},{2,6},{3,7},{4,8},{5,9},{6,10},{7,11},{8,12},{9,13},{1... | collective-permute-start | bytes 73736
Sparse Core Ops, SparseCore 0:
  9.5 41.0 all-gather.5
  52.8 50.6 all-gather.3
where the time goes:
time: 232 us; the launch traced here: 230 us
  other arithmetic  79.8 us (34%)
  blocking collectives  53.8 us (23%)
  local copies, waits for them, and re-layouts  46.4 us (20%)
  starting transfers between devices  17.2 us (7%)
  matrix products  16 us (7%)
  between operations  14.2 us (6%)
  waiting for transfers between devices  2.94 us (1%)
    unnamed x1, other arithmetic  79.8 us
    unnamed x14, local copies, waits for them, and re-layouts  31.8 us
    all_to_all x1, blocking collectives, body(): lax.all_to_all(query_right, 'query', split_axis=1, concat_axis=0, tiled=T...  27.9 us
    unnamed x1, blocking collectives  25.9 us
    unnamed x4, starting transfers between devices  17.1 us
    all_to_all x1, local copies, waits for them, and re-layouts, body(): lax.all_to_all(query_right, 'query', split_axis=1, concat_axis=0, tiled=T...  13.7 us
    dot_general x1, matrix products, body(): jnp.einsum('td,kdr->tkr', grad_out, lax.all_gather(query_left, 'query', a...  5.07 us
    dot_general x1, matrix products, body(): up = jnp.dot(whole, up_weight, preferred_element_type=jnp.float32)  4.93 us
  transfers between devices with their start and end apart: 6, of which 1 were waited for; matrix products, arithmetic and copies ran while one was open for 70% of the time, Pallas kernels for 0%

commit v1 on v0

--- a/solution.py
+++ b/solution.py
@@ -6,7 +6,9 @@
 
 def body(tokens, grad_out, gate_weight, up_weight, query_left, query_right):
     whole = lax.all_gather(tokens, "query", axis=0, tiled=True)
-    right_cols = lax.all_to_all(query_right, "query", split_axis=1, concat_axis=0, tiled=True)
+    pieces = jnp.split(query_right, lax.axis_size("query"), axis=1)
+    arrived = lax.all_to_all(jnp.stack(pieces), "query", 0, 0)
+    right_cols = jnp.concatenate(arrived, axis=0)
     right_wide = right_cols.astype(jnp.float32)
     num_queries = right_cols.shape[0]
     rank_size = right_cols.shape[2]

time: 232 us -> 137 us (0.59)
  other arithmetic: 79.8 us -> 0 us
  blocking collectives: 53.8 us -> 31 us
  waiting for transfers between devices: 2.94 us -> 25.2 us
  local copies, waits for them, and re-layouts: 46.4 us -> 27.4 us
  starting transfers between devices: 17.2 us -> 21.6 us
    unnamed x1 -> x0, other arithmetic: 79.8 us -> none
    all_to_all x1 -> x0, blocking collectives: 27.9 us -> none  [body(): lax.all_to_all(query_right, 'query', split_axis=1, concat_axis=0, tiled=T...]
    all_gather x1, waiting for transfers between devices: 0.02 us -> 22.3 us  [body(): whole = lax.all_gather(tokens, 'query', axis=0, tiled=True)]
    all_to_all x1 -> x0, local copies, waits for them, and re-layouts: 13.7 us -> none  [body(): lax.all_to_all(query_right, 'query', split_axis=1, concat_axis=0, tiled=T...]
    unnamed x14 -> x24, local copies, waits for them, and re-layouts: 31.8 us -> 25.2 us
    all_to_all x0 -> x1, starting transfers between devices: none -> 6.5 us  [body(): arrived = lax.all_to_all(jnp.stack(pieces), 'query', 0, 0)]
    unnamed x1, blocking collectives: 25.9 us -> 31 us
  transfers between devices with their start and end apart: 6 -> 7, of which waited for: 1 -> 2; matrix products, arithmetic and copies ran while one was open for 70% -> 51% of each run, Pallas kernels for 0% -> 0%
where the time goes in v1:
time: 137 us; the launch traced here: 136 us
  blocking collectives  31 us (23%)
  local copies, waits for them, and re-layouts  27.4 us (20%)
  waiting for transfers between devices  25.2 us (18%)
  starting transfers between devices  21.6 us (16%)
  matrix products  16.1 us (12%)
  between operations  14.2 us (10%)
    unnamed x1, blocking collectives  31 us
    unnamed x24, local copies, waits for them, and re-layouts  25.2 us
    all_gather x1, waiting for transfers between devices, body(): whole = lax.all_gather(tokens, 'query', axis=0, tiled=True)  22.3 us
    unnamed x4, starting transfers between devices  15.1 us
    all_to_all x1, starting transfers between devices, body(): arrived = lax.all_to_all(jnp.stack(pieces), 'query', 0, 0)  6.5 us
    dot_general x1, matrix products, body(): jnp.einsum('td,kdr->tkr', grad_out, lax.all_gather(query_left, 'query', a...  5.07 us
    dot_general x1, matrix products, body(): up = jnp.dot(whole, up_weight, preferred_element_type=jnp.float32)  4.97 us
    dot_general x1, matrix products, body(): gate = jnp.dot(whole, gate_weight, preferred_element_type=jnp.float32)  4.93 us
  transfers between devices with their start and end apart: 7, of which 2 were waited for; matrix products, arithmetic and copies ran while one was open for 51% of the time, Pallas kernels for 0%

profile of v1, /device:TPU:17, one launch (start us, length us, event | category | flops | bytes accessed | tf_op | source)
XLA Modules:
  0.0 135.6 jit_solution(7202075361333530947)
XLA Ops:
  6.5 0.0 copy-start
  6.5 0.0 all-gather.6.cloned.1.call-start
  6.5 0.7 all-gather.6.cloned.1.call-update
  7.3 0.0 all-gather.4.cloned.1.call-start
  7.3 0.7 all-gather.4.cloned.1.call-update
  8.0 1.4 %bitcast_dynamic-update-slice_fusion.15 = bf16[16,1,896,32]{2,3,1,0:T(8,128)(2,1)} fusion(bf16[1,14336,32]{1,2,0:T(8,128)(2,1)} %param.11), kind=kLoop, calls=%fused_computation.20 | loop fusion | bytes 114688
  9.5 1.4 %bitcast_dynamic-update-slice_fusion.14 = bf16[16,1,896,32]{2,3,1,0:T(8,128)(2,1)} fusion(bf16[16,1,896,32]{2,3,1,0:T(8,128)(2,1)} %bitcast_dynamic-update-slice_fusion.15, bf16[1,14336,32]{1,2,0:T(8,128)(2,1)} %param.11), kind=kLoop, calls=%fused_computation.19 | loop fusion | bytes 114688
  10.9 1.4 %bitcast_dynamic-update-slice_fusion.13 = bf16[16,1,896,32]{2,3,1,0:T(8,128)(2,1)} fusion(bf16[16,1,896,32]{2,3,1,0:T(8,128)(2,1)} %bitcast_dynamic-update-slice_fusion.14, bf16[1,14336,32]{1,2,0:T(8,128)(2,1)} %param.11), kind=kLoop, calls=%fused_computation.18 | loop fusion | bytes 114688
  12.3 1.4 %bitcast_dynamic-update-slice_fusion.12 = bf16[16,1,896,32]{2,3,1,0:T(8,128)(2,1)} fusion(bf16[16,1,896,32]{2,3,1,0:T(8,128)(2,1)} %bitcast_dynamic-update-slice_fusion.13, bf16[1,14336,32]{1,2,0:T(8,128)(2,1)} %param.11), kind=kLoop, calls=%fused_computation.17 | loop fusion | bytes 114688
  13.8 1.4 %bitcast_dynamic-update-slice_fusion.11 = bf16[16,1,896,32]{2,3,1,0:T(8,128)(2,1)} fusion(bf16[16,1,896,32]{2,3,1,0:T(8,128)(2,1)} %bitcast_dynamic-update-slice_fusion.12, bf16[1,14336,32]{1,2,0:T(8,128)(2,1)} %param.11), kind=kLoop, calls=%fused_computation.16 | loop fusion | bytes 114688
  15.2 1.4 %bitcast_dynamic-update-slice_fusion.10 = bf16[16,1,896,32]{2,3,1,0:T(8,128)(2,1)} fusion(bf16[16,1,896,32]{2,3,1,0:T(8,128)(2,1)} %bitcast_dynamic-update-slice_fusion.11, bf16[1,14336,32]{1,2,0:T(8,128)(2,1)} %param.11), kind=kLoop, calls=%fused_computation.15 | loop fusion | bytes 114688
  16.7 1.4 %bitcast_dynamic-update-slice_fusion.9 = bf16[16,1,896,32]{2,3,1,0:T(8,128)(2,1)} fusion(bf16[16,1,896,32]{2,3,1,0:T(8,128)(2,1)} %bitcast_dynamic-update-slice_fusion.10, bf16[1,14336,32]{1,2,0:T(8,128)(2,1)} %param.11), kind=kLoop, calls=%fused_computation.14 | loop fusion | bytes 114688
  18.1 1.4 %bitcast_dynamic-update-slice_fusion.8 = bf16[16,1,896,32]{2,3,1,0:T(8,128)(2,1)} fusion(bf16[16,1,896,32]{2,3,1,0:T(8,128)(2,1)} %bitcast_dynamic-update-slice_fusion.9, bf16[1,14336,32]{1,2,0:T(8,128)(2,1)} %param.11), kind=kLoop, calls=%fused_computation.13 | loop fusion | bytes 114688
  19.5 1.4 %bitcast_dynamic-update-slice_fusion.7 = bf16[16,1,896,32]{2,3,1,0:T(8,128)(2,1)} fusion(bf16[16,1,896,32]{2,3,1,0:T(8,128)(2,1)} %bitcast_dynamic-update-slice_fusion.8, bf16[1,14336,32]{1,2,0:T(8,128)(2,1)} %param.11), kind=kLoop, calls=%fused_computation.12 | loop fusion | bytes 114688
  21.0 1.4 %bitcast_dynamic-update-slice_fusion.6 = bf16[16,1,896,32]{2,3,1,0:T(8,128)(2,1)} fusion(bf16[16,1,896,32]{2,3,1,0:T(8,128)(2,1)} %bitcast_dynamic-update-slice_fusion.7, bf16[1,14336,32]{1,2,0:T(8,128)(2,1)} %param.11), kind=kLoop, calls=%fused_computation.11 | loop fusion | bytes 114688
  22.4 1.4 %bitcast_dynamic-update-slice_fusion.5 = bf16[16,1,896,32]{2,3,1,0:T(8,128)(2,1)} fusion(bf16[16,1,896,32]{2,3,1,0:T(8,128)(2,1)} %bitcast_dynamic-update-slice_fusion.6, bf16[1,14336,32]{1,2,0:T(8,128)(2,1)} %param.11), kind=kLoop, calls=%fused_computation.10 | loop fusion | bytes 114688
  23.9 1.4 %bitcast_dynamic-update-slice_fusion.4 = bf16[16,1,896,32]{2,3,1,0:T(8,128)(2,1)} fusion(bf16[16,1,896,32]{2,3,1,0:T(8,128)(2,1)} %bitcast_dynamic-update-slice_fusion.5, bf16[1,14336,32]{1,2,0:T(8,128)(2,1)} %param.11), kind=kLoop, calls=%fused_computation.9 | loop fusion | bytes 114688
  25.3 1.4 %bitcast_dynamic-update-slice_fusion.3 = bf16[16,1,896,32]{2,3,1,0:T(8,128)(2,1)} fusion(bf16[16,1,896,32]{2,3,1,0:T(8,128)(2,1)} %bitcast_dynamic-update-slice_fusion.4, bf16[1,14336,32]{1,2,0:T(8,128)(2,1)} %param.11), kind=kLoop, calls=%fused_computation.8 | loop fusion | bytes 114688
  26.8 1.4 %bitcast_dynamic-update-slice_fusion.2 = bf16[16,1,896,32]{2,3,1,0:T(8,128)(2,1)} fusion(bf16[16,1,896,32]{2,3,1,0:T(8,128)(2,1)} %bitcast_dynamic-update-slice_fusion.3, bf16[1,14336,32]{1,2,0:T(8,128)(2,1)} %param.11), kind=kLoop, calls=%fused_computation.7 | loop fusion | bytes 114688
  28.2 1.4 %bitcast_dynamic-update-slice_fusion.1 = bf16[16,1,896,32]{2,3,1,0:T(8,128)(2,1)} fusion(bf16[16,1,896,32]{2,3,1,0:T(8,128)(2,1)} %bitcast_dynamic-update-slice_fusion.2, bf16[1,14336,32]{1,2,0:T(8,128)(2,1)} %param.11), kind=kLoop, calls=%fused_computation.6 | loop fusion | bytes 114688
  29.6 1.5 %bitcast_dynamic-update-slice_fusion = bf16[16,1,896,32]{2,3,1,0:T(8,128)(2,1)} fusion(bf16[16,1,896,32]{2,3,1,0:T(8,128)(2,1)} %bitcast_dynamic-update-slice_fusion.1, bf16[1,14336,32]{1,2,0:T(8,128)(2,1)} %param.11), kind=kLoop, calls=%fused_computation.5 | loop fusion | bytes 114688 | tf_op jit(solution)/shard_map/stack | solution.py:10
  31.1 6.5 %all-to-all-start = ((bf16[16,1,896,32]{2,3,1,0:T(8,128)(2,1)}), bf16[16,1,896,32]{2,3,1,0:T(8,128)(2,1)S(1)}, u32[]{:S(2)}, u32[]{:S(2)}) async-start(bf16[16,1,896,32]{2,3,1,0:T(8,128)(2,1)} %bitcast_dynamic-update-slice_fusion), calls=%async_computation | async-start | bytes 1835008 | tf_op jit(solution)/shard_map/all_to_all | solution.py:10
  37.6 22.3 %all-gather.6.cloned.1.call-done = bf16[16,12,4096]{2,1,0:T(8,128)(2,1)} async-done(((bf16[1,12,4096]{2,1,0:T(8,128)(2,1)}), bf16[16,12,4096]{2,1,0:T(8,128)(2,1)}) %all-gather.6.cloned.1.call-update) | async-done | bytes 1572880 | tf_op jit(solution)/shard_map/all_gather | solution.py:8
  59.9 2.5 %reshape.11 = bf16[192,4096]{1,0:T(8,128)(2,1)S(1)} reshape(bf16[16,12,4096]{2,1,0:T(8,128)(2,1)} %all-gather.6.cloned.1.call-done) | data formatting | bytes 3145728
  62.3 4.9 %fusion.4 = f32[192,896]{1,0:T(8,128)S(1)} fusion(bf16[192,4096]{1,0:T(8,128)(2,1)S(1)} %reshape.11, bf16[4096,896]{1,0:T(8,128)(2,1)} %param.8), kind=kOutput, calls=%fused_computation.22 | convolution fusion | flops 1409286144 | bytes 9601024 | tf_op jit(solution)/shard_map/dot_general | solution.py:16
  67.3 0.0 copy-start.1
  67.3 5.0 %convolution_multiply_fusion = f32[192,896]{1,0:T(8,128)S(1)} fusion(bf16[192,4096]{1,0:T(8,128)(2,1)S(1)} %reshape.11, bf16[4096,896]{1,0:T(8,128)(2,1)} %param.9, f32[192,896]{1,0:T(8,128)S(1)} %fusion.4), kind=kOutput, calls=%fused_computation | convolution fusion | flops 1410146304 | bytes 10289152 | tf_op jit(solution)/shard_map/dot_general | solution.py:17
  72.3 0.0 all-to-all-done
  72.3 1.1 fusion.5
  73.4 31.0 %fusion = f32[16,512]{1,0:T(8,128)S(1)} fusion(f32[192,512]{1,0:T(8,128)S(1)} %fusion.5), kind=kCustom, calls=%all-reduce-scatter | all-reduce-scatter fusion | flops 131073 | bytes 426496
  104.4 2.8 %collective-permute-start = (f32[16,512]{1,0:T(8,128)S(1)}, f32[16,512]{1,0:T(8,128)S(1)}, u32[]{:S(2)}, u32[]{:S(2)}) collective-permute-start(f32[16,512]{1,0:T(8,128)S(1)} %fusion), channel_id=1, source_target_pairs={{0,1},{1,2},{2,3},{3,4},{4,5},{5,6},{6,7},{7,8},{8,9},{9,10},{10,1... | collective-permute-start | bytes 98312
  107.2 2.9 %collective-permute-start.1 = (f32[16,512]{1,0:T(8,128)S(1)}, f32[16,512]{1,0:T(8,128)S(1)}, u32[]{:S(2)}, u32[]{:S(2)}) collective-permute-start(f32[16,512]{1,0:T(8,128)S(1)} %fusion), channel_id=1, source_target_pairs={{0,2},{1,3},{2,4},{3,5},{4,6},{5,7},{6,8},{7,9},{8,10},{9,11},{10,... | collective-permute-start | bytes 98312
  110.1 7.5 %collective-permute-start.2 = (f32[16,512]{1,0:T(8,128)S(1)}, f32[16,512]{1,0:T(8,128)S(1)}, u32[]{:S(2)}, u32[]{:S(2)}) collective-permute-start(f32[16,512]{1,0:T(8,128)S(1)} %fusion), channel_id=1, source_target_pairs={{0,3},{1,4},{2,5},{3,6},{4,7},{5,8},{6,9},{7,10},{8,11},{9,12},{10... | collective-permute-start | bytes 98312
  117.6 1.9 %collective-permute-start.3 = (f32[12,512]{1,0:T(8,128)S(1)}, f32[12,512]{1,0:T(8,128)S(1)}, u32[]{:S(2)}, u32[]{:S(2)}) collective-permute-start(f32[12,512]{1,0:T(8,128)S(1)} %slice), channel_id=1, source_target_pairs={{0,4},{1,5},{2,6},{3,7},{4,8},{5,9},{6,10},{7,11},{8,12},{9,13},{1... | collective-permute-start | bytes 73736
  119.6 0.0 copy-done.1
  119.6 0.6 dynamic-slice.4
  120.8 1.5 %collective-permute-done.3 = f32[12,512]{1,0:T(8,128)S(1)} collective-permute-done((f32[12,512]{1,0:T(8,128)S(1)}, f32[12,512]{1,0:T(8,128)S(1)}, u32[]{:S(2)}, u32[]{:S(2)}) %collective-permute-start.3) | collective-permute-done | bytes 24608
  122.3 0.0 collective-permute-done
  122.3 0.0 collective-permute-done.1
  122.3 0.0 collective-permute-done.2
  122.3 0.5 concatenate
  122.8 0.1 reshape.9
  122.9 0.0 all-gather.4.cloned.1.call-done
  122.9 0.0 copy-done
  123.0 5.1 %fusion.3 = f32[12,16]{0,1:T(8,128)S(1)} fusion(f32[12,16,32]{2,1,0:T(8,128)S(1)} %reshape.9, bf16[16,4096,32]{1,2,0:T(8,128)(2,1)} %all-gather.4.cloned.1.call-done, bf16[12,4096]{1,0:T(8,128)(2,1)S(1)} %copy-done), kind=kOutput, calls=%fused_computation.4 | convolution fusion | flops 50343744 | bytes 4317952 | tf_op jit(solution)/shard_map/td,kdr->tkr/dot_general | solution.py:27
  128.0 0.7 copy.9
  (2 shorter events, 0.0 us)
Async XLA Ops:
  6.5 116.4 %copy-start = (bf16[12,4096]{1,0:T(8,128)(2,1)S(1)}, bf16[12,4096]{1,0:T(8,128)(2,1)}, u32[]{:S(2)}) copy-start(bf16[12,4096]{1,0:T(8,128)(2,1)} %param.7) | copy-start | bytes 294916
  6.5 53.4 %all-gather.6.cloned.1.call-start = ((), (), s32[]{:S(2)}) async-start(), calls=%async_computation.2 | async-start | bytes 2228224 | tf_op jit(solution)/shard_map/all_gather | solution.py:8
  7.3 115.7 %all-gather.4.cloned.1.call-start = ((), (), s32[]{:S(2)}) async-start(), calls=%async_computation.1 | async-start | bytes 4456448 | tf_op jit(solution)/shard_map/all_gather | solution.py:30
  31.1 41.2 %all-to-all-start = ((bf16[16,1,896,32]{2,3,1,0:T(8,128)(2,1)}), bf16[16,1,896,32]{2,3,1,0:T(8,128)(2,1)S(1)}, u32[]{:S(2)}, u32[]{:S(2)}) async-start(bf16[16,1,896,32]{2,3,1,0:T(8,128)(2,1)} %bitcast_dynamic-update-slice_fusion), calls=%async_computation | async-start | bytes 1835008 | tf_op jit(solution)/shard_map/all_to_all | solution.py:10
  67.3 52.3 %copy-start.1 = (u32[32]{0:T(128)S(1)}, u32[32]{0:T(128)}, u32[]{:S(2)}) copy-start(u32[32]{0:T(128)} %constant.11) | copy-start | bytes 388
  104.4 17.9 %collective-permute-start = (f32[16,512]{1,0:T(8,128)S(1)}, f32[16,512]{1,0:T(8,128)S(1)}, u32[]{:S(2)}, u32[]{:S(2)}) collective-permute-start(f32[16,512]{1,0:T(8,128)S(1)} %fusion), channel_id=1, source_target_pairs={{0,1},{1,2},{2,3},{3,4},{4,5},{5,6},{6,7},{7,8},{8,9},{9,10},{10,1... | collective-permute-start | bytes 98312
  107.2 15.1 %collective-permute-start.1 = (f32[16,512]{1,0:T(8,128)S(1)}, f32[16,512]{1,0:T(8,128)S(1)}, u32[]{:S(2)}, u32[]{:S(2)}) collective-permute-start(f32[16,512]{1,0:T(8,128)S(1)} %fusion), channel_id=1, source_target_pairs={{0,2},{1,3},{2,4},{3,5},{4,6},{5,7},{6,8},{7,9},{8,10},{9,11},{10,... | collective-permute-start | bytes 98312
  110.1 12.2 %collective-permute-start.2 = (f32[16,512]{1,0:T(8,128)S(1)}, f32[16,512]{1,0:T(8,128)S(1)}, u32[]{:S(2)}, u32[]{:S(2)}) collective-permute-start(f32[16,512]{1,0:T(8,128)S(1)} %fusion), channel_id=1, source_target_pairs={{0,3},{1,4},{2,5},{3,6},{4,7},{5,8},{6,9},{7,10},{8,11},{9,12},{10... | collective-permute-start | bytes 98312
  117.6 4.7 %collective-permute-start.3 = (f32[12,512]{1,0:T(8,128)S(1)}, f32[12,512]{1,0:T(8,128)S(1)}, u32[]{:S(2)}, u32[]{:S(2)}) collective-permute-start(f32[12,512]{1,0:T(8,128)S(1)} %slice), channel_id=1, source_target_pairs={{0,4},{1,5},{2,6},{3,7},{4,8},{5,9},{6,10},{7,11},{8,12},{9,13},{1... | collective-permute-start | bytes 73736
Sparse Core Ops, SparseCore 0:
  9.5 50.3 all-gather.5
  62.0 54.0 all-gather.3
